TPU v7x, 256 devices: a whole 4x4x8 slice. The times are simulated.
256 devices in a mesh: grp: 2 (over x_lo), tok: 8 (over x_hi, y), voc: 16 (over z, core).
Axes of the slice: x: 4 (x_hi: 2, x_lo: 2; x = x_hi * 2 + x_lo), y: 4, z: 8, core: 2. Of those that a mesh axis runs over, the one named last changes fastest.
Arguments:
- hidden: bfloat16 [2, 512, 4096], P('grp', 'tok'), may hold values from -110 to 110
- head: bfloat16 [2, 4096, 81920], P('grp', None, ('tok', 'voc')), may hold values from -0.09375 to 0.09375
- teacher: bfloat16 [512, 81920], P('grp', ('tok', 'voc')), may hold values from -250 to 250
- labels: int32 [512], P('grp'), may hold values from 0 to 81919
Outputs:
- hidden_grad: bfloat16 [2, 512, 4096], P('grp', ('tok', 'voc'))
- head_grad: bfloat16 [2, 4096, 81920], P('grp', None, ('tok', 'voc'))
All inputs are finite; a program needn't handle non-finite values.
Results may differ from a plain program's by a relative error of at most 0.0034.
Values may be sent and summed in bfloat16 or wider, within the bound.
A program may use at most 128 MiB of HBM per device.

v0:
```python
import jax
import jax.numpy as jnp
from jax import lax
from jax.sharding import PartitionSpec as P

grad_scale = 32.0
kl_weight = 0.5


def body(hidden, head, teacher, labels):
    all_rows = lax.all_gather(hidden[0], "tok", axis=0, tiled=True)
    teacher_all, labels_all = (
        lax.all_gather(teacher, "grp", axis=0, tiled=True),
        lax.all_gather(labels, "grp", axis=0, tiled=True),
    )
    weights = head[0]
    columns = weights.shape[1]
    logits = jnp.dot(all_rows, weights, preferred_element_type=jnp.float32)
    teacher_vals = teacher_all.astype(jnp.float32)
    student_top, teacher_top = lax.pmax(
        (jnp.max(logits, axis=1), jnp.max(teacher_vals, axis=1)), ("tok", "voc")
    )
    student_exp = jnp.exp(logits - student_top[:, None])
    teacher_exp = jnp.exp(teacher_vals - teacher_top[:, None])
    student_total, teacher_total = lax.psum(
        (jnp.sum(student_exp, axis=1), jnp.sum(teacher_exp, axis=1)), ("tok", "voc")
    )
    student_prob = student_exp / student_total[:, None]
    teacher_prob = teacher_exp / teacher_total[:, None]
    column_base = lax.axis_index(("tok", "voc")) * columns
    column_ids = column_base + jnp.arange(columns, dtype=jnp.int32)
    onehot = (column_ids[None, :] == labels_all[:, None]).astype(jnp.float32)
    grad = (
        grad_scale * (student_prob - kl_weight * teacher_prob - (1.0 - kl_weight) * onehot)
    ).astype(jnp.bfloat16)
    head_out = lax.dot_general(
        all_rows, grad, (((0,), (0,)), ((), ())), preferred_element_type=jnp.float32
    )
    hidden_out = lax.psum_scatter(
        lax.dot_general(
            grad, weights, (((1,), (1,)), ((), ())), preferred_element_type=jnp.float32
        ),
        ("tok", "voc"),
        scatter_dimension=0,
        tiled=True,
    )
    return (hidden_out[None].astype(jnp.bfloat16), head_out[None].astype(jnp.bfloat16))


def solution(mesh):
    placed = (
        P("grp", "tok", None),
        P("grp", None, ("tok", "voc")),
        P("grp", ("tok", "voc")),
        P("grp"),
    )
    return jax.shard_map(
        body,
        mesh=mesh,
        in_specs=placed,
        out_specs=(P("grp", ("tok", "voc"), None), P("grp", None, ("tok", "voc"))),
        check_vma=False,
    )
```

profile of v0, /device:TPU:1, one launch (start us, length us, event | category | flops | bytes accessed | tf_op | source)
XLA Modules:
  0.0 1505.0 jit_solution(12255452402862927322)
XLA Ops:
  7.2 0.0 copy-start
  7.2 0.0 all-gather.4.cloned.1.call-start
  7.2 0.7 all-gather.4.cloned.1.call-update
  7.9 1.3 dynamic-slice
  9.8 9.1 all_gather.10
  18.9 0.2 reduce_max.24
  19.1 0.0 copy-done
  19.1 3.7 all-gather.1
  22.8 67.7 %all-gather.4.cloned.1.call-done = bf16[1,512,4096]{2,1,0:T(8,128)(2,1)} async-done(((bf16[1,64,4096]{2,1,0:T(8,128)(2,1)}), bf16[1,512,4096]{2,1,0:T(8,128)(2,1)}) %all-gather.4.cloned.1.call-update) | async-done | bytes 4194320 | tf_op jit(solution)/shard_map/all_gather | solution.py:11
  90.5 6.9 fusion.10
  97.5 324.1 %all-reduce.2 = (f32[512]{0:T(512)S(1)}, f32[512]{0:T(512)S(1)}) all-reduce(bf16[512]{0:T(512)(128)(2,1)S(1)} %reduce_max.24, f32[512]{0:T(512)S(1)} %get-tuple-element.10), channel_id=1, replica_groups=mesh['grp'=2,'tok'=8,'voc'=16] {'tok','voc'}, use_global_device_ids=true, to_apply=%region_5.0 | all-reduce | flops 1024 | bytes 7168 | tf_op jit(solution)/shard_map/pmax | solution.py:20
  421.6 0.7 fusion.7
  422.4 326.3 %all-reduce.1 = (f32[512]{0:T(512)S(1)}, f32[512]{0:T(512)S(1)}) all-reduce(f32[512]{0:T(512)S(1)} %get-tuple-element.12, f32[512]{0:T(512)S(1)} %get-tuple-element.13), channel_id=1, replica_groups=mesh['grp'=2,'tok'=8,'voc'=16] {'tok','voc'}, use_global_device_ids=true, to_apply=%region_7.0 | all-reduce | flops 1024 | bytes 8192 | tf_op jit(solution)/shard_map/psum | solution.py:25
  748.7 0.0 copy-start.1
  748.7 8.9 fusion.1
  757.6 0.0 copy-done.1
  757.6 5.9 fusion
  763.5 7.8 copy.7
  771.3 725.4 %all-reduce.4 = bf16[512,4096]{1,0:T(8,128)(2,1)} all-reduce(f32[512,4096]{1,0:T(8,128)} %fusion.1), channel_id=3, replica_groups=mesh['grp'=2,'tok'=8,'voc'=16] {'tok','voc'}, use_global_device_ids=true, to_apply=%region_8.0.clone | all-reduce | flops 2097152 | bytes 12582912
  1496.7 1.5 fusion.9
  (1 shorter events, 0.0 us)
Async XLA Ops:
  7.2 11.9 copy-start
  7.2 83.4 %all-gather.4.cloned.1.call-start = ((), (), s32[]{:S(2)}) async-start(), calls=%async_computation | async-start | bytes 4718592 | tf_op jit(solution)/shard_map/all_gather | solution.py:11
  748.7 8.9 copy-start.1
Sparse Core Ops, SparseCore 0:
  10.7 79.8 all-gather.3
where the time goes:
time: 1510 us
  blocking collectives  1390 us (92%)
  waiting for transfers between devices  68.4 us (5%)
  matrix products  21.7 us (1%)
    unnamed x1, blocking collectives  725 us
    psum x1, blocking collectives, body(): lax.psum((jnp.sum(student_exp, axis=1), jnp.sum(teacher_exp, axis=1)), ('...  326 us
    pmax x1, blocking collectives, body(): lax.pmax((jnp.max(logits, axis=1), jnp.max(teacher_vals, axis=1)), ('tok'...  324 us
    all_gather x1, waiting for transfers between devices, body(): all_rows = lax.all_gather(hidden[0], 'tok', axis=0, tiled=True)  67.7 us
  transfers between devices with their start and end apart: 1, of which 1 were waited for; matrix products, arithmetic and copies ran while one was open for 0% of the time, Pallas kernels for 0%

commit v1 on v0

v1 whole, which is shorter than its diff:
```python
import functools

import jax
import jax.numpy as jnp
from jax import lax
from jax.experimental import pallas as pl
from jax.experimental.pallas import tpu as pltpu
from jax.sharding import PartitionSpec as P

GRAD_SCALE = 32.0
KL_WEIGHT = 0.5
MESH = pl.DeviceIdType.MESH
F32 = jnp.float32
BF16 = jnp.bfloat16

NY = 4
NZ = 8
TOK = 2 * NY
VOC = 2 * NZ
ROWS = 64
HALF = NY * ROWS
TOKENS = 2 * HALF
COLS = 640
WIDE = 256
DHALF = 8 * WIDE


def spread(row):
    return jnp.broadcast_to(row, (128, 128)).T


def as_row(col):
    return jnp.broadcast_to(col, (128, 128)).T[0:1, :]


def merge(parts):
    tops = parts[:, 0:4, :]
    top = jnp.max(tops, axis=0)
    total = jnp.sum(parts[:, 4:8, :] * jnp.exp(tops - top[None]), axis=0)
    return jnp.concatenate([top, total], axis=0)


def kernel(
    hid_in, teach_in, lab_in, head_in, hg_out, ho_out,
    hid, head_v, head_sib, teach_sib, lab_sib, prob, base, grad_own, grad_sib,
    t_voc, t_tok, t_fin, s_voc, s_tok,
    part, ya_buf, qa_own, qa_send, xa_buf, xb_buf, qb, yb_buf, red, z_buf, fin_own, fin_sib, ho_buf,
    head_sem, ho_sem, g_s, g_r, ga_s, ga_r, gb_s, gb_r, d_s, d_r, misc_s, misc_r,
    tv_s, tv_r, tt_s, tt_r, sv_s, sv_r, st_s, st_r, gr_s, gr_r,
    ya_s, ya_r, xa_s, xa_r, xb_s, xb_r, yb_s, yb_r, z_s, z_r,
):
    g = lax.axis_index("grp")
    t = lax.axis_index("tok")
    v = lax.axis_index("voc")
    xh, y = t // NY, t % NY
    z, c = v // 2, v % 2
    sib = (g, t, z * 2 + (1 - c))
    xpart = (g, (1 - xh) * NY + y, v)
    gpart = (1 - g, t, v)

    def ydev(r):
        return (g, xh * NY + lax.rem(y + r, NY), v)

    def zdev(r):
        return (g, t, lax.rem(z + r, NZ) * 2 + c)

    def vdev(r):
        return (g, t, lax.rem(v + r, VOC))

    def tdev(r):
        return (g, lax.rem(t + r, TOK), v)

    def yfrom(r):
        return lax.rem(y + NY - r, NY)

    def rdma(src, dst, ss, rs, device):
        return pltpu.make_async_remote_copy(
            src_ref=src, dst_ref=dst, send_sem=ss, recv_sem=rs, device_id=device, device_id_type=MESH
        )

    def rows_of(col, yy):
        return pl.ds(pl.multiple_of((col * NY + yy) * ROWS, ROWS), ROWS)

    def head_copy(i):
        rows = pl.ds(i * 1024, 1024)
        return pltpu.make_async_copy(head_in.at[rows, :], head_v.at[rows, :], head_sem.at[i])

    for i in range(4):
        head_copy(i).start()

    barrier = pltpu.get_barrier_semaphore()
    for r in range(1, VOC):
        pl.semaphore_signal(barrier, inc=1, device_id=vdev(r), device_id_type=MESH)
    for r in range(1, TOK):
        pl.semaphore_signal(barrier, inc=1, device_id=tdev(r), device_id_type=MESH)
    pl.semaphore_signal(barrier, inc=1, device_id=gpart, device_id_type=MESH)

    own_rows = rows_of(xh, y)
    for k in range(16):
        hid[k, own_rows, :] = hid_in[:, k * WIDE : (k + 1) * WIDE]

    zero_row = jnp.zeros((1, 128), F32)
    tops, sums = [], []
    for b in range(2):
        vals = teach_in[b * 128 : (b + 1) * 128, :].astype(F32)
        top = jnp.max(vals, axis=1, keepdims=True)
        tops.append(as_row(top))
        sums.append(as_row(jnp.sum(jnp.exp(vals - top), axis=1, keepdims=True)))
    t_voc[0] = jnp.concatenate(tops + [zero_row, zero_row] + sums + [zero_row, zero_row], axis=0)

    pl.semaphore_wait(barrier, VOC + TOK - 1)

    own_chunks = pl.ds(pl.multiple_of(c * 8, 8), 8)
    a_chunks = pl.ds(pl.multiple_of(c * 8, 4), 4)
    b_chunks = pl.ds(pl.multiple_of(c * 8 + 4, 4), 4)

    def gather_first(r):
        here = hid.at[own_chunks, own_rows, :]
        return rdma(here, here, g_s.at[r], g_r.at[r], xpart if r == 0 else ydev(r))

    def gather_first_in(r):
        here = hid.at[own_chunks, rows_of(1 - xh, y) if r == 0 else rows_of(xh, yfrom(r)), :]
        return rdma(here, here, g_s.at[r], g_r.at[r], sib)

    def forward_a(r):
        here = hid.at[a_chunks, rows_of(1 - xh, y), :]
        return rdma(here, here, ga_s.at[r], ga_r.at[r], ydev(r))

    def forward_a_in(r):
        here = hid.at[a_chunks, rows_of(1 - xh, yfrom(r)), :]
        return rdma(here, here, ga_s.at[r], ga_r.at[r], sib)

    def forward_b(r):
        here = hid.at[b_chunks, rows_of(xh, yfrom(r)), :]
        return rdma(here, here, gb_s.at[r], gb_r.at[r], xpart)

    def forward_b_in(r):
        here = hid.at[b_chunks, rows_of(1 - xh, yfrom(r)), :]
        return rdma(here, here, gb_s.at[r], gb_r.at[r], sib)

    def to_sibling(i, core):
        if i == 0:
            part_at, rows = pl.ds(pl.multiple_of(core * 8, 8), 8), rows_of(1 - xh, y)
        elif i < 4:
            part_at, rows = pl.ds(pl.multiple_of(core * 8, 8), 8), rows_of(xh, yfrom(i))
        elif i < 7:
            part_at, rows = pl.ds(pl.multiple_of(core * 8, 4), 4), rows_of(1 - xh, yfrom(i - 3))
        else:
            part_at, rows = pl.ds(pl.multiple_of(core * 8 + 4, 4), 4), rows_of(1 - xh, yfrom(i - 6))
        here = hid.at[part_at, rows, :]
        return rdma(here, here, d_s.at[i], d_r.at[i], sib)

    def stat_voc(buf, ss, rs, r):
        return rdma(buf.at[0], buf.at[r], ss.at[r], rs.at[r], vdev(r))

    def stat_tok(buf, ss, rs, r):
        return rdma(buf.at[0], buf.at[r], ss.at[r], rs.at[r], tdev(r))

    for r in (0, 1, 3, 2):
        gather_first(r).start()
    for r in range(1, VOC):
        stat_voc(t_voc, tv_s, tv_r, r).start()

    sib_rows = pl.ds(pl.multiple_of((1 - c) * DHALF, DHALF), DHALF)
    head_swap = rdma(head_in.at[sib_rows, :], head_sib, misc_s.at[0], misc_r.at[0], sib)
    head_swap.start()
    lab_swap = rdma(lab_in, lab_sib, misc_s.at[1], misc_r.at[1], gpart)
    lab_swap.start()
    teach_swap = rdma(teach_in, teach_sib, misc_s.at[2], misc_r.at[2], gpart)

    gather_first_in(0).wait_recv()
    for r in (1, 3, 2):
        forward_a(r).start()
    to_sibling(0, c).start()
    for r in (1, 3, 2):
        gather_first_in(r).wait_recv()
        forward_b(r).start()
        to_sibling(r, c).start()
    teach_swap.start()

    for r in range(1, VOC):
        stat_voc(t_voc, tv_s, tv_r, r).wait_recv()
    t_tok[0] = merge(t_voc[...])
    for r in range(1, TOK):
        stat_tok(t_tok, tt_s, tt_r, r).start()

    for i in range(4):
        head_copy(i).wait()

    def logits_of(col):
        rows = pl.ds(pl.multiple_of(col * HALF, HALF), HALF)
        lhs = jnp.concatenate([hid[k, rows, :] for k in range(16)], axis=1)
        logits = jnp.dot(lhs, head_v[...], preferred_element_type=F32)
        top = jnp.max(logits, axis=1, keepdims=True)
        expo = jnp.exp(logits - top)
        prob[rows, :] = expo
        total = jnp.sum(expo, axis=1, keepdims=True)
        for b in range(2):
            at = slice(b * 128, (b + 1) * 128)
            s_voc[0, pl.ds(col * 2 + b, 1), :] = as_row(top[at])
            s_voc[0, pl.ds(4 + col * 2 + b, 1), :] = as_row(total[at])

    def logits_step(i, carry):
        @pl.when(i == 0)
        def _():
            for r in (1, 3, 2):
                to_sibling(r, 1 - c).wait_recv()

        @pl.when(i == 1)
        def _():
            to_sibling(0, 1 - c).wait_recv()
            for r in (1, 3, 2):
                forward_a_in(r).wait_recv()
                to_sibling(3 + r, c).start()
            for r in (1, 3, 2):
                forward_b_in(r).wait_recv()
                to_sibling(6 + r, c).start()
            for r in (1, 3, 2):
                to_sibling(3 + r, 1 - c).wait_recv()
                to_sibling(6 + r, 1 - c).wait_recv()

        logits_of(jnp.where(i == 0, xh, 1 - xh))
        return carry

    lax.fori_loop(0, 2, logits_step, 0)

    for r in range(1, VOC):
        stat_voc(s_voc, sv_s, sv_r, r).start()

    for r in range(1, TOK):
        stat_tok(t_tok, tt_s, tt_r, r).wait_recv()
    t_fin[0] = merge(t_tok[...])
    fin_swap = rdma(t_fin.at[0], t_fin.at[1], misc_s.at[3], misc_r.at[3], gpart)
    fin_swap.start()
    lab_swap.wait_recv()
    teach_swap.wait_recv()
    fin_swap.wait_recv()
    column_base = (t * VOC + v) * COLS
    for which in range(2):
        values = teach_in if which == 0 else teach_sib
        labels = lab_in if which == 0 else lab_sib
        row0 = (g if which == 0 else 1 - g) * 256
        for b in range(2):
            rows = pl.ds(pl.multiple_of(row0 + b * 128, 128), 128)
            top = spread(t_fin[which, b : b + 1, :])
            scale = KL_WEIGHT / spread(t_fin[which, 4 + b : 5 + b, :])
            label = spread(labels[b : b + 1, :])
            for n in range(COLS // 128):
                at = slice(n * 128, (n + 1) * 128)
                soft = jnp.exp(values[b * 128 : (b + 1) * 128, at].astype(F32) - top) * scale
                ids = column_base + n * 128 + lax.broadcasted_iota(jnp.int32, (128, 128), 1)
                base[rows, at] = soft + jnp.where(ids == label, 1.0 - KL_WEIGHT, 0.0)

    for r in range(1, VOC):
        stat_voc(s_voc, sv_s, sv_r, r).wait_recv()
    s_tok[0] = merge(s_voc[...])
    for r in range(1, TOK):
        stat_tok(s_tok, st_s, st_r, r).start()
    for r in range(1, TOK):
        stat_tok(s_tok, st_s, st_r, r).wait_recv()
    final = merge(s_tok[...])
    factor = jnp.exp(s_voc[0, 0:4, :] - final[0:4, :]) / final[4:8, :]

    def grad_swap(b):
        rows = pl.ds(b * 128, 128)
        return rdma(grad_own.at[rows, :], grad_sib.at[rows, :], gr_s.at[b], gr_r.at[b], sib)

    for b in range(4):
        rows = slice(b * 128, (b + 1) * 128)
        mat = spread(factor[b : b + 1, :])
        for n in range(COLS // 128):
            at = slice(n * 128, (n + 1) * 128)
            grad_own[rows, at] = (GRAD_SCALE * (prob[rows, at] * mat - base[rows, at])).astype(BF16)
        grad_swap(b).start()
    head_swap.wait_recv()
    for b in range(4):
        grad_swap(b).wait_recv()

    def product(j):
        lhs = jnp.concatenate([grad_own[...], grad_sib[...]], axis=1)
        own = head_v[pl.ds(pl.multiple_of(c * DHALF + j * WIDE, WIDE), WIDE), :]
        other = head_sib[pl.ds(pl.multiple_of(j * WIDE, WIDE), WIDE), :]
        rhs = jnp.concatenate([own, other], axis=1)
        out = lax.dot_general(lhs, rhs, (((1,), (1,)), ((), ())), preferred_element_type=F32)
        part[j] = out.astype(BF16).reshape(2, NY, ROWS, WIDE)

    def send_ya(i, r):
        return rdma(
            part.at[i, :, lax.rem(y + r, NY)], ya_buf.at[i, r - 1], ya_s.at[i, r], ya_r.at[i, r], ydev(r)
        )

    def send_xb(i):
        return rdma(part.at[4 + i, 1 - xh], xb_buf.at[i], xb_s.at[i], xb_r.at[i], xpart)

    def send_xa(i):
        return rdma(qa_send.at[i], xa_buf.at[i], xa_s.at[i], xa_r.at[i], xpart)

    def send_yb(i, r):
        return rdma(qb.at[i, lax.rem(y + r, NY)], yb_buf.at[i, r - 1], yb_s.at[i, r], yb_r.at[i, r], ydev(r))

    def send_z(i, r):
        rows = pl.ds(pl.multiple_of(lax.rem(z + r, NZ) * 8, 8), 8)
        return rdma(red.at[i, :, rows, :], z_buf.at[i, r - 1], z_s.at[i, r], z_r.at[i, r], zdev(r))

    def ho_copy(k):
        return pltpu.make_async_copy(
            ho_buf.at[k], ho_out.at[pl.ds(pl.multiple_of(k * WIDE, WIDE), WIDE), :], ho_sem.at[k]
        )

    def head_piece(k):
        out = lax.dot_general(
            hid[k], grad_own[...], (((0,), (0,)), ((), ())), preferred_element_type=F32
        )
        ho_buf[k] = out.astype(BF16)
        ho_copy(k).start()

    def step1(i, carry):
        product(i)
        for r in (1, 3, 2):
            send_ya(i, r).start()
        product(4 + i)
        send_xb(i).start()
        return carry

    lax.fori_loop(0, 4, step1, 0)

    def step2(i, carry):
        head_piece(2 * i)
        head_piece(2 * i + 1)
        for r in (1, 3, 2):
            send_ya(i, r).wait_recv()

        def column(col):
            total = part[i, col, y].astype(F32)
            for r in range(3):
                total = total + ya_buf[i, r, col].astype(F32)
            return total

        qa_own[i] = column(xh)
        qa_send[i] = column(1 - xh).astype(BF16)
        send_xa(i).start()
        send_xb(i).wait_recv()
        qb[i] = (part[4 + i, xh].astype(F32) + xb_buf[i].astype(F32)).astype(BF16)
        for r in (1, 3, 2):
            send_yb(i, r).start()
        return carry

    lax.fori_loop(0, 4, step2, 0)

    def step3(i, carry):
        head_piece(8 + 2 * i)
        head_piece(9 + 2 * i)
        send_xa(i).wait_recv()
        red[i, 0] = qa_own[i] + xa_buf[i].astype(F32)
        for r in (1, 3, 2):
            send_yb(i, r).wait_recv()
        total = qb[i, y].astype(F32)
        for r in range(3):
            total = total + yb_buf[i, r].astype(F32)
        red[i, 1] = total
        for r in (4, 3, 5, 2, 6, 1, 7):
            send_z(i, r).start()
        return carry

    lax.fori_loop(0, 4, step3, 0)

    def step4(i, carry):
        for r in range(1, NZ):
            send_z(i, r).wait_recv()
        rows = pl.ds(pl.multiple_of(z * 8, 8), 8)
        total = red[i, :, rows, :]
        for r in range(NZ - 1):
            total = total + z_buf[i, r]
        fin_own[:, i] = total
        return carry

    lax.fori_loop(0, 4, step4, 0)
    fin_core = rdma(fin_own, fin_sib, misc_s.at[4], misc_r.at[4], sib)
    fin_core.start()
    fin_core.wait_recv()
    first = c == 0
    for j in range(8):
        own = fin_own[j // 4, j % 4]
        other = fin_sib[j // 4, j % 4]
        own = jnp.where(first, own[0:4], own[4:8])
        other = jnp.where(first, other[0:4], other[4:8])
        low = jnp.where(first, own, other)
        high = jnp.where(first, other, own)
        hg_out[:, j * WIDE : (j + 1) * WIDE] = low.astype(BF16)
        hg_out[:, DHALF + j * WIDE : DHALF + (j + 1) * WIDE] = high.astype(BF16)

    for r in range(4):
        gather_first(r).wait_send()
    for r in range(1, 4):
        forward_a(r).wait_send()
        forward_b(r).wait_send()
    for i in range(10):
        to_sibling(i, c).wait_send()
    for r in range(1, VOC):
        stat_voc(t_voc, tv_s, tv_r, r).wait_send()
        stat_voc(s_voc, sv_s, sv_r, r).wait_send()
    for r in range(1, TOK):
        stat_tok(t_tok, tt_s, tt_r, r).wait_send()
        stat_tok(s_tok, st_s, st_r, r).wait_send()
    for copy in (head_swap, lab_swap, teach_swap, fin_swap, fin_core):
        copy.wait_send()
    for b in range(4):
        grad_swap(b).wait_send()

    def drain(i, carry):
        for r in range(1, 4):
            send_ya(i, r).wait_send()
            send_yb(i, r).wait_send()
        send_xa(i).wait_send()
        send_xb(i).wait_send()
        for r in range(1, NZ):
            send_z(i, r).wait_send()
        return carry

    lax.fori_loop(0, 4, drain, 0)

    def drain_head(k, carry):
        ho_copy(k).wait()
        return carry

    lax.fori_loop(0, 16, drain_head, 0)


def body(hidden, head, teacher, labels):
    dma = pltpu.SemaphoreType.DMA
    scratch = [
        pltpu.VMEM((16, TOKENS, WIDE), BF16),
        pltpu.VMEM((16 * WIDE, COLS), BF16),
        pltpu.VMEM((DHALF, COLS), BF16),
        pltpu.VMEM((256, COLS), BF16),
        pltpu.VMEM((2, 128), jnp.int32),
        pltpu.VMEM((TOKENS, COLS), F32),
        pltpu.VMEM((TOKENS, COLS), F32),
        pltpu.VMEM((TOKENS, COLS), BF16),
        pltpu.VMEM((TOKENS, COLS), BF16),
        pltpu.VMEM((VOC, 8, 128), F32),
        pltpu.VMEM((TOK, 8, 128), F32),
        pltpu.VMEM((2, 8, 128), F32),
        pltpu.VMEM((VOC, 8, 128), F32),
        pltpu.VMEM((TOK, 8, 128), F32),
        pltpu.VMEM((8, 2, NY, ROWS, WIDE), BF16),
        pltpu.VMEM((4, 3, 2, ROWS, WIDE), BF16),
        pltpu.VMEM((4, ROWS, WIDE), F32),
        pltpu.VMEM((4, ROWS, WIDE), BF16),
        pltpu.VMEM((4, ROWS, WIDE), BF16),
        pltpu.VMEM((4, NY, ROWS, WIDE), BF16),
        pltpu.VMEM((4, NY, ROWS, WIDE), BF16),
        pltpu.VMEM((4, 3, ROWS, WIDE), BF16),
        pltpu.VMEM((4, 2, ROWS, WIDE), F32),
        pltpu.VMEM((4, NZ - 1, 2, 8, WIDE), F32),
        pltpu.VMEM((2, 4, 8, WIDE), F32),
        pltpu.VMEM((2, 4, 8, WIDE), F32),
        pltpu.VMEM((16, WIDE, COLS), BF16),
        dma((4,)), dma((16,)),
        dma((4,)), dma((4,)), dma((4,)), dma((4,)), dma((4,)), dma((4,)),
        dma((10,)), dma((10,)), dma((5,)), dma((5,)),
        dma((VOC,)), dma((VOC,)), dma((TOK,)), dma((TOK,)),
        dma((VOC,)), dma((VOC,)), dma((TOK,)), dma((TOK,)),
        dma((4,)), dma((4,)),
        dma((4, 4)), dma((4, 4)), dma((4,)), dma((4,)),
        dma((4,)), dma((4,)), dma((4, 4)), dma((4, 4)),
        dma((4, NZ)), dma((4, NZ)),
    ]
    vmem = pl.BlockSpec(memory_space=pltpu.VMEM)
    hbm = pl.BlockSpec(memory_space=pl.ANY)
    hidden_out, head_out = pl.pallas_call(
        kernel,
        out_shape=(
            jax.ShapeDtypeStruct((4, 16 * WIDE), BF16),
            jax.ShapeDtypeStruct((16 * WIDE, COLS), BF16),
        ),
        in_specs=[vmem, vmem, vmem, hbm],
        out_specs=(vmem, hbm),
        scratch_shapes=scratch,
        compiler_params=pltpu.CompilerParams(
            collective_id=0, has_side_effects=True, vmem_limit_bytes=56 << 20
        ),
    )(hidden[0], teacher, labels.reshape(2, 128), head[0])
    return hidden_out[None], head_out[None]


def solution(mesh):
    placed = (
        P("grp", "tok", None),
        P("grp", None, ("tok", "voc")),
        P("grp", ("tok", "voc")),
        P("grp"),
    )
    return jax.shard_map(
        body,
        mesh=mesh,
        in_specs=placed,
        out_specs=(P("grp", ("tok", "voc"), None), P("grp", None, ("tok", "voc"))),
        check_vma=False,
    )
```

time: 1510 us -> 92.4 us (0.06)
  blocking collectives: 1390 us -> 0 us
  Pallas kernels: 0 us -> 84.9 us
  waiting for transfers between devices: 68.4 us -> 0 us
  matrix products: 21.7 us -> 0 us
    unnamed x1 -> x0, blocking collectives: 725 us -> none
    psum x1 -> x0, blocking collectives: 326 us -> none  [body(): lax.psum((jnp.sum(student_exp, axis=1), jnp.sum(teacher_exp, axis=1)), ('...]
    pmax x1 -> x0, blocking collectives: 324 us -> none  [body(): lax.pmax((jnp.max(logits, axis=1), jnp.max(teacher_vals, axis=1)), ('tok'...]
    pallas_call x0 -> x1, Pallas kernels: none -> 84.9 us  [body(): pl.pallas_call(kernel, out_shape=(jax.ShapeDtypeStruct((4, 16 * WIDE), BF...]
    all_gather x1 -> x0, waiting for transfers between devices: 67.7 us -> none  [body(): all_rows = lax.all_gather(hidden[0], 'tok', axis=0, tiled=True)]
    dot_general x3 -> x0, matrix products: 21.7 us -> none  [the longest x1 8.9 us: body(): lax.dot_general(grad, weights, (((1,), (1,)), ((), ())), preferred_elemen...]
  transfers between devices with their start and end apart: 1 -> 0, of which waited for: 1 -> 0; matrix products, arithmetic and copies ran while one was open for 0% -> 0% of each run, Pallas kernels for 0% -> 0%
where the time goes in v1:
time: 92.4 us; the launch traced here: 92.2 us
  Pallas kernels  84.9 us (92%)
  local copies, waits for them, and re-layouts  6.68 us (7%)
    pallas_call x1, Pallas kernels, body(): pl.pallas_call(kernel, out_shape=(jax.ShapeDtypeStruct((4, 16 * WIDE), BF...  84.9 us
    unnamed x2, local copies, waits for them, and re-layouts  6.68 us

profile of v1, /device:TPU:1, one launch (start us, length us, event | category | flops | bytes accessed | tf_op | source)
XLA Modules:
  0.0 92.2 jit_solution(16122026124080553635)
XLA Ops:
  0.6 84.9 %shard_map.59 = (bf16[4,4096]{1,0:T(4,128)(2,1)}, bf16[4096,640]{1,0:T(8,128)(2,1)}) custom-call(bf16[64,4096]{1,0:T(8,128)(2,1)} %bitcast.7, bf16[256,640]{1,0:T(8,128)(2,1)} %teach_in.1, s32[2,128]{1,0:T(2,128)} %bitcast.9, bf16[4096,640]{1,0:T(8,128)(2,1)} %bitcast.5), custom_call_target="tpu_custom_call" | custom-call | tf_op jit(solution)/shard_map/pallas_call | solution.py:471
  85.5 1.4 %copy.8 = bf16[1,4,4096]{2,1,0:T(4,128)(2,1)} copy(bf16[1,4,4096]{2,1,0:T(4,128)(2,1)} %bitcast.8) | data formatting | bytes 65536
  86.9 5.3 %copy.9 = bf16[1,4096,640]{2,1,0:T(8,128)(2,1)} copy(bf16[1,4096,640]{2,1,0:T(8,128)(2,1)} %bitcast.6) | data formatting | bytes 10485760

commit v2 on v0

v2 whole, which is shorter than its diff:
```python
import functools

import jax
import jax.numpy as jnp
from jax import lax
from jax.experimental import pallas as pl
from jax.experimental.pallas import tpu as pltpu
from jax.sharding import PartitionSpec as P

GRAD_SCALE = 32.0
KL_WEIGHT = 0.5
MESH = pl.DeviceIdType.MESH
F32 = jnp.float32
BF16 = jnp.bfloat16

NY = 4
NZ = 8
TOK = 2 * NY
VOC = 2 * NZ
ROWS = 64
HALF = NY * ROWS
TOKENS = 2 * HALF
COLS = 640
WIDE = 256
DHALF = 8 * WIDE


def spread(row):
    return jnp.broadcast_to(row, (128, 128)).T


def as_row(col):
    return jnp.broadcast_to(col, (128, 128)).T[0:1, :]


def merge(parts):
    tops = parts[:, 0:4, :]
    top = jnp.max(tops, axis=0)
    total = jnp.sum(parts[:, 4:8, :] * jnp.exp(tops - top[None]), axis=0)
    return jnp.concatenate([top, total], axis=0)


def kernel(
    hid_hbm, teach_hbm, lab_hbm, head_hbm, hg_out, ho_out,
    hid_in, teach_own, lab_own, hid, head_v, head_sib, teach_sib, lab_sib, prob, base, grad,
    t_voc, t_tok, t_fin, s_voc, s_tok,
    part, own, pair_buf, ya_buf, qa_own, qa_send, xa_buf, xb_buf, qb, qb_own, yb_buf, red, z_buf,
    fin_own, fin_sib, ho_buf,
    in_sem, ho_sem, h_s, h_r, misc_s, misc_r, tv_s, tv_r, tt_s, tt_r, sv_s, sv_r, st_s, st_r, pr_s, pr_r,
    pair_s, pair_r, ya_s, ya_r, xa_s, xa_r, xb_s, xb_r, yb_s, yb_r, z_s, z_r,
):
    g = lax.axis_index("grp")
    t = lax.axis_index("tok")
    v = lax.axis_index("voc")
    xh, y = t // NY, t % NY
    z, c = v // 2, v % 2
    parity = z % 2
    sib = (g, t, z * 2 + (1 - c))
    xpart = (g, (1 - xh) * NY + y, v)
    gpart = (1 - g, t, v)

    def ydev(r):
        return (g, xh * NY + lax.rem(y + r, NY), v)

    def zdev(r):
        return (g, t, lax.rem(z + r, NZ) * 2 + c)

    def vdev(r):
        return (g, t, lax.rem(v + r, VOC))

    def tdev(r):
        return (g, lax.rem(t + r, TOK), v)

    def yfrom(r):
        return lax.rem(y + NY - r, NY)

    def rdma(src, dst, ss, rs, device):
        return pltpu.make_async_remote_copy(
            src_ref=src, dst_ref=dst, send_sem=ss, recv_sem=rs, device_id=device, device_id_type=MESH
        )

    def rows_of(col, yy):
        return pl.ds(pl.multiple_of((col * NY + yy) * ROWS, ROWS), ROWS)

    barrier = pltpu.get_barrier_semaphore()
    for r in range(1, VOC):
        pl.semaphore_signal(barrier, inc=1, device_id=vdev(r), device_id_type=MESH)
    for r in range(1, TOK):
        pl.semaphore_signal(barrier, inc=1, device_id=tdev(r), device_id_type=MESH)
    pl.semaphore_signal(barrier, inc=1, device_id=gpart, device_id_type=MESH)

    loads = [
        pltpu.make_async_copy(hid_hbm, hid_in, in_sem.at[0]),
        pltpu.make_async_copy(teach_hbm, teach_own, in_sem.at[1]),
        pltpu.make_async_copy(lab_hbm, lab_own, in_sem.at[2]),
    ]
    for i in range(4):
        rows = pl.ds(i * 1024, 1024)
        loads.append(pltpu.make_async_copy(head_hbm.at[rows, :], head_v.at[rows, :], in_sem.at[3 + i]))
    for load in loads:
        load.start()

    own_rows = rows_of(xh, y)
    loads[0].wait()
    for k in range(16):
        hid[k, own_rows, :] = hid_in[:, k * WIDE : (k + 1) * WIDE]
    loads[1].wait()
    loads[2].wait()

    zero_row = jnp.zeros((1, 128), F32)
    tops, sums = [], []
    for b in range(2):
        vals = teach_own[b * 128 : (b + 1) * 128, :].astype(F32)
        top = jnp.max(vals, axis=1, keepdims=True)
        tops.append(as_row(top))
        sums.append(as_row(jnp.sum(jnp.exp(vals - top), axis=1, keepdims=True)))
    t_voc[0] = jnp.concatenate(tops + [zero_row, zero_row] + sums + [zero_row, zero_row], axis=0)

    pl.semaphore_wait(barrier, VOC + TOK - 1)

    sends = []

    def go(here, device):
        i = len(sends)
        copy = rdma(here, here, h_s.at[i], h_r.at[i], device)
        copy.start()
        sends.append(copy)
        return copy

    first = c * 8 + parity * 4
    other = c * 8 + (1 - parity) * 4

    def chunks(start, n):
        return pl.ds(pl.multiple_of(start, 2), n)

    x_in = go(hid.at[chunks(first, 4), own_rows, :], xpart)
    y_in = {r: go(hid.at[chunks(first, 4), own_rows, :], ydev(r)) for r in (1, 3, 2)}

    def stat_voc(buf, ss, rs, r):
        return rdma(buf.at[0], buf.at[r], ss.at[r], rs.at[r], vdev(r))

    def stat_tok(buf, ss, rs, r):
        return rdma(buf.at[0], buf.at[r], ss.at[r], rs.at[r], tdev(r))

    for r in range(1, VOC):
        stat_voc(t_voc, tv_s, tv_r, r).start()
    sib_rows = pl.ds(pl.multiple_of((1 - c) * DHALF, DHALF), DHALF)
    head_swap = rdma(head_hbm.at[sib_rows, :], head_sib, misc_s.at[0], misc_r.at[0], sib)
    head_swap.start()
    lab_swap = rdma(lab_own, lab_sib, misc_s.at[1], misc_r.at[1], gpart)
    lab_swap.start()
    teach_swap = rdma(teach_own, teach_sib, misc_s.at[2], misc_r.at[2], gpart)

    near, far, z_in = [], [], []

    def share(start, n, rows, arrivals):
        arrivals.append(go(hid.at[chunks(start, n), rows, :], sib))

    def along_z(rows, arrivals, up, down):
        if up:
            copy = go(hid.at[chunks(first, 2), rows, :], zdev(1))
            z_in.append((copy, other, rows, arrivals))
        if down:
            copy = go(hid.at[chunks(first + 2, 2), rows, :], zdev(NZ - 1))
            z_in.append((copy, other + 2, rows, arrivals))

    x_in.wait_recv()
    mirror = rows_of(1 - xh, y)
    a_in = {r: go(hid.at[chunks(first, 2), mirror, :], ydev(r)) for r in (1, 3, 2)}
    along_z(mirror, far, True, True)
    share(first, 4, mirror, far)
    b_in = {}
    for r in (1, 3, 2):
        y_in[r].wait_recv()
        rows = rows_of(xh, yfrom(r))
        b_in[r] = go(hid.at[chunks(first + 2, 2), rows, :], xpart)
        along_z(rows, near, True, True)
        share(first, 4, rows, near)
    teach_swap.start()
    for r in range(1, VOC):
        stat_voc(t_voc, tv_s, tv_r, r).wait_recv()
    t_tok[0] = merge(t_voc[...])
    for r in range(1, TOK):
        stat_tok(t_tok, tt_s, tt_r, r).start()
    for r in (1, 3, 2):
        rows = rows_of(1 - xh, yfrom(r))
        a_in[r].wait_recv()
        along_z(rows, far, True, False)
        share(first, 2, rows, far)
        b_in[r].wait_recv()
        along_z(rows, far, False, True)
        share(first + 2, 2, rows, far)
    for r in range(1, TOK):
        stat_tok(t_tok, tt_s, tt_r, r).wait_recv()
    t_fin[0] = merge(t_tok[...])
    fin_swap = rdma(t_fin.at[0], t_fin.at[1], misc_s.at[3], misc_r.at[3], gpart)
    fin_swap.start()
    for copy, start, rows, arrivals in z_in:
        copy.wait_recv()
        share(start, 2, rows, arrivals)
    for load in loads[3:]:
        load.wait()

    def prob_swap(i, col):
        here = prob.at[c, pl.ds(pl.multiple_of(col * HALF, HALF), HALF), :]
        return rdma(here, here, pr_s.at[i], pr_r.at[i], sib)

    def logits_step(i, carry):
        @pl.when(i == 0)
        def _():
            for copy in near:
                copy.wait_recv()

        @pl.when(i == 1)
        def _():
            for copy in far:
                copy.wait_recv()

        col = jnp.where(i == 0, xh, 1 - xh)
        rows = pl.ds(pl.multiple_of(col * HALF, HALF), HALF)
        lhs = jnp.concatenate([hid[k, rows, :] for k in range(16)], axis=1)
        logits = jnp.dot(lhs, head_v[...], preferred_element_type=F32)
        top = jnp.max(logits, axis=1, keepdims=True)
        expo = jnp.exp(logits - top)
        prob[c, rows, :] = expo
        prob_swap(i, col).start()
        total = jnp.sum(expo, axis=1, keepdims=True)
        for b in range(2):
            at = slice(b * 128, (b + 1) * 128)
            s_voc[0, pl.ds(col * 2 + b, 1), :] = as_row(top[at])
            s_voc[0, pl.ds(4 + col * 2 + b, 1), :] = as_row(total[at])
        return carry

    lax.fori_loop(0, 2, logits_step, 0)

    for r in range(1, VOC):
        stat_voc(s_voc, sv_s, sv_r, r).start()

    lab_swap.wait_recv()
    teach_swap.wait_recv()
    fin_swap.wait_recv()
    column_base = (t * VOC + v) * COLS
    base_swaps = []
    for which in range(2):
        values = teach_own if which == 0 else teach_sib
        labels = lab_own if which == 0 else lab_sib
        row0 = (g if which == 0 else 1 - g) * 256
        for b in range(2):
            rows = pl.ds(pl.multiple_of(row0 + b * 128, 128), 128)
            top = spread(t_fin[which, b : b + 1, :])
            scale = KL_WEIGHT / spread(t_fin[which, 4 + b : 5 + b, :])
            label = spread(labels[b : b + 1, :])
            for n in range(COLS // 128):
                at = slice(n * 128, (n + 1) * 128)
                soft = jnp.exp(values[b * 128 : (b + 1) * 128, at].astype(F32) - top) * scale
                ids = column_base + n * 128 + lax.broadcasted_iota(jnp.int32, (128, 128), 1)
                base[c, rows, at] = soft + jnp.where(ids == label, 1.0 - KL_WEIGHT, 0.0)
        here = base.at[c, pl.ds(pl.multiple_of(row0, 256), 256), :]
        base_swaps.append(rdma(here, here, pr_s.at[2 + which], pr_r.at[2 + which], sib))
        base_swaps[-1].start()

    for r in range(1, VOC):
        stat_voc(s_voc, sv_s, sv_r, r).wait_recv()
    s_tok[0] = merge(s_voc[...])
    for r in range(1, TOK):
        stat_tok(s_tok, st_s, st_r, r).start()
    head_swap.wait_recv()
    prob_swap(0, xh).wait_recv()
    prob_swap(1, 1 - xh).wait_recv()
    for copy in base_swaps:
        copy.wait_recv()
    for r in range(1, TOK):
        stat_tok(s_tok, st_s, st_r, r).wait_recv()
    final = merge(s_tok[...])
    sib_slot = jnp.where(c == 1, 1, VOC - 1)
    for which in range(2):
        tops = s_voc[0, 0:4, :] if which == 0 else s_voc[sib_slot, 0:4, :]
        core = c if which == 0 else 1 - c
        factor = jnp.exp(tops - final[0:4, :]) / final[4:8, :]
        for b in range(4):
            rows = slice(b * 128, (b + 1) * 128)
            mat = spread(factor[b : b + 1, :])
            for n in range(COLS // 128):
                at = slice(n * 128, (n + 1) * 128)
                out = GRAD_SCALE * (prob[core, rows, at] * mat - base[core, rows, at])
                grad[rows, which * COLS + n * 128 : which * COLS + (n + 1) * 128] = out.astype(BF16)

    def chunk_of(i):
        return jnp.where(i < 2, (1 - parity) * 2 + i, jnp.where(i < 6, i + 2, parity * 2 + i - 6))

    def send_pair(i):
        return rdma(part.at[i], pair_buf.at[i], pair_s.at[i], pair_r.at[i], zdev(1 if i == 0 else NZ - 1))

    def send_ya(k, r):
        return rdma(
            part.at[2 + 2 * k, :, lax.rem(y + r, NY)], ya_buf.at[k, r - 1], ya_s.at[k, r], ya_r.at[k, r], ydev(r)
        )

    def send_xb(k):
        return rdma(part.at[3 + 2 * k, 1 - xh], xb_buf.at[k], xb_s.at[k], xb_r.at[k], xpart)

    def send_xa(k):
        return rdma(qa_send.at[k], xa_buf.at[k], xa_s.at[k], xa_r.at[k], xpart)

    def send_yb(k, r):
        return rdma(qb.at[k, lax.rem(y + r, NY)], yb_buf.at[k, r - 1], yb_s.at[k, r], yb_r.at[k, r], ydev(r))

    def send_z(k, r):
        rows = pl.ds(pl.multiple_of(lax.rem(z + r, NZ) * 8, 8), 8)
        return rdma(red.at[k, :, rows, :], z_buf.at[k, r - 1], z_s.at[k, r], z_r.at[k, r], zdev(r))

    def ho_copy(k):
        return pltpu.make_async_copy(
            ho_buf.at[k], ho_out.at[pl.ds(pl.multiple_of(k * WIDE, WIDE), WIDE), :], ho_sem.at[k]
        )

    def head_pieces(start, n):
        def piece(k, carry):
            out = lax.dot_general(
                hid[k], grad[:, 0:COLS], (((0,), (0,)), ((), ())), preferred_element_type=F32
            )
            ho_buf[k] = out.astype(BF16)
            ho_copy(k).start()
            return carry

        lax.fori_loop(start, start + n, piece, 0)

    def product(i, carry):
        j = chunk_of(i)
        left = head_v[pl.ds(pl.multiple_of(c * DHALF + j * WIDE, WIDE), WIDE), :]
        right = head_sib[pl.ds(pl.multiple_of(j * WIDE, WIDE), WIDE), :]
        rhs = jnp.concatenate([left, right], axis=1)
        out = lax.dot_general(grad[...], rhs, (((1,), (1,)), ((), ())), preferred_element_type=F32)
        out = out.reshape(2, NY, ROWS, WIDE)
        own[i] = out
        part[i] = out.astype(BF16)

        for n in range(2):

            @pl.when(i == n)
            def _():
                send_pair(n).start()

            @pl.when(i == 2 + 2 * n)
            def _():
                for r in (1, 3, 2):
                    send_ya(n, r).start()

            @pl.when(i == 3 + 2 * n)
            def _():
                send_xb(n).start()

        return carry

    lax.fori_loop(0, 8, product, 0)

    def second(k, carry):
        for r in (1, 3, 2):
            send_ya(k, r).wait_recv()

        def column(col):
            total = own[2 + 2 * k, col, y]
            for r in range(3):
                total = total + ya_buf[k, r, col].astype(F32)
            return total

        qa_send[k] = column(1 - xh).astype(BF16)
        send_xa(k).start()
        qa_own[k] = column(xh)
        send_xb(k).wait_recv()
        qb[k] = (own[3 + 2 * k, xh] + xb_buf[k].astype(F32)).astype(BF16)
        for r in (1, 3, 2):
            send_yb(k, r).start()
        qb_own[k] = own[3 + 2 * k, xh, y] + xb_buf[k, y].astype(F32)
        return carry

    def third(k, carry):
        send_xa(k).wait_recv()
        red[k, 0] = qa_own[k] + xa_buf[k].astype(F32)
        for r in (1, 3, 2):
            send_yb(k, r).wait_recv()
        total = qb_own[k]
        for r in range(3):
            total = total + yb_buf[k, r].astype(F32)
        red[k, 1] = total
        for r in (4, 3, 5, 2, 6, 1, 7):
            send_z(k, r).start()
        return carry

    head_pieces(0, 4)
    lax.fori_loop(0, 2, second, 0)
    for n in range(2):
        send_pair(n).wait_recv()
        total = own[6 + n] + pair_buf[n].astype(F32)
        own[6 + n] = total
        part[6 + n] = total.astype(BF16)
        if n == 0:
            for r in (1, 3, 2):
                send_ya(2, r).start()
        else:
            send_xb(2).start()
    head_pieces(4, 4)
    lax.fori_loop(0, 2, third, 0)
    head_pieces(8, 4)
    lax.fori_loop(2, 3, second, 0)
    head_pieces(12, 4)
    lax.fori_loop(2, 3, third, 0)

    z_rows = pl.ds(pl.multiple_of(z * 8, 8), 8)
    for k in range(3):
        for r in range(1, NZ):
            send_z(k, r).wait_recv()
        total = red[k, :, z_rows, :]
        for r in range(1, NZ) if k < 2 else (2, 4, 6):
            total = total + z_buf[k, r - 1]
        if k < 2:
            fin_own[4 + 2 * k] = total[0]
            fin_own[5 + 2 * k] = total[1]
        else:
            fin_own[parity * 2] = total[0]
            fin_own[parity * 2 + 1] = total[1]
            total = z_buf[k, 0] + z_buf[k, 2] + z_buf[k, 4] + z_buf[k, 6]
            fin_own[(1 - parity) * 2] = total[0]
            fin_own[(1 - parity) * 2 + 1] = total[1]
    fin_core = rdma(fin_own, fin_sib, misc_s.at[4], misc_r.at[4], sib)
    fin_core.start()
    fin_core.wait_recv()
    lower = c == 0
    for j in range(8):
        mine = jnp.where(lower, fin_own[j, 0:4], fin_own[j, 4:8])
        theirs = jnp.where(lower, fin_sib[j, 0:4], fin_sib[j, 4:8])
        hg_out[:, j * WIDE : (j + 1) * WIDE] = jnp.where(lower, mine, theirs).astype(BF16)
        hg_out[:, DHALF + j * WIDE : DHALF + (j + 1) * WIDE] = jnp.where(lower, theirs, mine).astype(BF16)

    for copy in sends + base_swaps + [head_swap, lab_swap, teach_swap, fin_swap, fin_core]:
        copy.wait_send()
    prob_swap(0, xh).wait_send()
    prob_swap(1, 1 - xh).wait_send()
    for r in range(1, VOC):
        stat_voc(t_voc, tv_s, tv_r, r).wait_send()
        stat_voc(s_voc, sv_s, sv_r, r).wait_send()
    for r in range(1, TOK):
        stat_tok(t_tok, tt_s, tt_r, r).wait_send()
        stat_tok(s_tok, st_s, st_r, r).wait_send()
    for n in range(2):
        send_pair(n).wait_send()

    def drain(k, carry):
        for r in range(1, 4):
            send_ya(k, r).wait_send()
            send_yb(k, r).wait_send()
        send_xa(k).wait_send()
        send_xb(k).wait_send()
        for r in range(1, NZ):
            send_z(k, r).wait_send()
        return carry

    lax.fori_loop(0, 3, drain, 0)

    def drain_head(k, carry):
        ho_copy(k).wait()
        return carry

    lax.fori_loop(0, 16, drain_head, 0)


def body(hidden, head, teacher, labels):
    dma = pltpu.SemaphoreType.DMA
    i32 = jnp.int32
    vmem = pltpu.VMEM
    scratch = [
        vmem((ROWS, 16 * WIDE), BF16), vmem((256, COLS), BF16), vmem((2, 128), i32),
        vmem((16, TOKENS, WIDE), BF16),
        vmem((16 * WIDE, COLS), BF16), vmem((DHALF, COLS), BF16),
        vmem((256, COLS), BF16), vmem((2, 128), i32),
        vmem((2, TOKENS, COLS), F32), vmem((2, TOKENS, COLS), F32),
        vmem((TOKENS, 2 * COLS), BF16),
        vmem((VOC, 8, 128), F32), vmem((TOK, 8, 128), F32), vmem((2, 8, 128), F32),
        vmem((VOC, 8, 128), F32), vmem((TOK, 8, 128), F32),
        vmem((8, 2, NY, ROWS, WIDE), BF16), vmem((8, 2, NY, ROWS, WIDE), F32),
        vmem((2, 2, NY, ROWS, WIDE), BF16),
        vmem((3, 3, 2, ROWS, WIDE), BF16),
        vmem((3, ROWS, WIDE), F32), vmem((3, ROWS, WIDE), BF16), vmem((3, ROWS, WIDE), BF16),
        vmem((3, NY, ROWS, WIDE), BF16), vmem((3, NY, ROWS, WIDE), BF16),
        vmem((3, ROWS, WIDE), F32), vmem((3, 3, ROWS, WIDE), BF16),
        vmem((3, 2, ROWS, WIDE), F32), vmem((3, NZ - 1, 2, 8, WIDE), F32),
        vmem((8, 8, WIDE), F32), vmem((8, 8, WIDE), F32),
        vmem((16, WIDE, COLS), BF16),
        dma((7,)), dma((16,)), dma((48,)), dma((48,)), dma((5,)), dma((5,)),
        dma((VOC,)), dma((VOC,)), dma((TOK,)), dma((TOK,)),
        dma((VOC,)), dma((VOC,)), dma((TOK,)), dma((TOK,)),
        dma((4,)), dma((4,)), dma((2,)), dma((2,)),
        dma((3, 4)), dma((3, 4)), dma((3,)), dma((3,)),
        dma((3,)), dma((3,)), dma((3, 4)), dma((3, 4)),
        dma((3, NZ)), dma((3, NZ)),
    ]
    hbm = pl.BlockSpec(memory_space=pltpu.HBM)
    hidden_out, head_out = pl.pallas_call(
        kernel,
        out_shape=(
            jax.ShapeDtypeStruct((4, 16 * WIDE), BF16),
            jax.ShapeDtypeStruct((16 * WIDE, COLS), BF16),
        ),
        in_specs=[hbm] * 4,
        out_specs=(pl.BlockSpec(memory_space=pltpu.VMEM), pl.BlockSpec(memory_space=pl.ANY)),
        scratch_shapes=scratch,
        compiler_params=pltpu.CompilerParams(
            collective_id=0, has_side_effects=True, vmem_limit_bytes=44 << 20
        ),
    )(hidden[0], teacher, labels.reshape(2, 128), head[0])
    return hidden_out[None], head_out[None]


def solution(mesh):
    placed = (
        P("grp", "tok", None),
        P("grp", None, ("tok", "voc")),
        P("grp", ("tok", "voc")),
        P("grp"),
    )
    return jax.shard_map(
        body,
        mesh=mesh,
        in_specs=placed,
        out_specs=(P("grp", ("tok", "voc"), None), P("grp", None, ("tok", "voc"))),
        check_vma=False,
    )
```

time: 1510 us -> 83.8 us (0.06)
  blocking collectives: 1390 us -> 0 us
  Pallas kernels: 0 us -> 77.3 us
  waiting for transfers between devices: 68.4 us -> 0 us
  matrix products: 21.7 us -> 0 us
    unnamed x1 -> x0, blocking collectives: 725 us -> none
    psum x1 -> x0, blocking collectives: 326 us -> none  [body(): lax.psum((jnp.sum(student_exp, axis=1), jnp.sum(teacher_exp, axis=1)), ('...]
    pmax x1 -> x0, blocking collectives: 324 us -> none  [body(): lax.pmax((jnp.max(logits, axis=1), jnp.max(teacher_vals, axis=1)), ('tok'...]
    pallas_call x0 -> x1, Pallas kernels: none -> 77.3 us  [body(): pl.pallas_call(kernel, out_shape=(jax.ShapeDtypeStruct((4, 16 * WIDE), BF...]
    all_gather x1 -> x0, waiting for transfers between devices: 67.7 us -> none  [body(): all_rows = lax.all_gather(hidden[0], 'tok', axis=0, tiled=True)]
    dot_general x3 -> x0, matrix products: 21.7 us -> none  [the longest x1 8.9 us: body(): lax.dot_general(grad, weights, (((1,), (1,)), ((), ())), preferred_elemen...]
  transfers between devices with their start and end apart: 1 -> 0, of which waited for: 1 -> 0; matrix products, arithmetic and copies ran while one was open for 0% -> 0% of each run, Pallas kernels for 0% -> 0%
where the time goes in v2:
time: 83.8 us; the launch traced here: 83.6 us
  Pallas kernels  77.3 us (92%)
  local copies, waits for them, and re-layouts  5.66 us (7%)
    pallas_call x1, Pallas kernels, body(): pl.pallas_call(kernel, out_shape=(jax.ShapeDtypeStruct((4, 16 * WIDE), BF...  77.3 us
    unnamed x8, local copies, waits for them, and re-layouts  5.66 us

profile of v2, /device:TPU:1, one launch (start us, length us, event | category | flops | bytes accessed | tf_op | source)
XLA Modules:
  0.0 83.6 jit_solution(32062146870220726)
XLA Ops:
  0.6 0.0 copy-start
  0.6 1.0 %copy-done = bf16[1,64,4096]{2,1,0:T(8,128)(2,1)S(1)} copy-done((bf16[1,64,4096]{2,1,0:T(8,128)(2,1)S(1)}, bf16[1,64,4096]{2,1,0:T(8,128)(2,1)}, u32[]{:S(2)}) %copy-start) | copy-done | bytes 524312
  1.7 0.0 copy-start.1
  1.7 1.0 %copy-done.1 = bf16[256,640]{1,0:T(8,128)(2,1)S(1)} copy-done((bf16[256,640]{1,0:T(8,128)(2,1)S(1)}, bf16[256,640]{1,0:T(8,128)(2,1)}, u32[]{:S(2)}) %copy-start.1) | copy-done | bytes 327704
  2.6 0.0 copy-start.2
  2.6 0.7 copy-done.2
  3.3 77.3 %shard_map.59 = (bf16[4,4096]{1,0:T(4,128)(2,1)S(1)}, bf16[4096,640]{1,0:T(8,128)(2,1)S(1)}) custom-call(bf16[64,4096]{1,0:T(8,128)(2,1)S(1)} %bitcast.6, bf16[256,640]{1,0:T(8,128)(2,1)S(1)} %copy-done.1, s32[2,128]{1,0:T(2,128)S(1)} %bitcast.8, bf16[4096,640]{1,0:T(8,128)(2,1)} %bitcast.9), custom_call_target="tpu_custom_call" | custom-call | tf_op jit(solution)/shard_map/pallas_call | solution.py:498
  80.7 0.6 copy.8
  81.3 2.4 %copy.9 = bf16[1,4096,640]{2,1,0:T(8,128)(2,1)} copy(bf16[1,4096,640]{2,1,0:T(8,128)(2,1)S(1)} %bitcast.5) | data formatting | bytes 10485760
Async XLA Ops:
  0.6 1.0 %copy-start = (bf16[1,64,4096]{2,1,0:T(8,128)(2,1)S(1)}, bf16[1,64,4096]{2,1,0:T(8,128)(2,1)}, u32[]{:S(2)}) copy-start(bf16[1,64,4096]{2,1,0:T(8,128)(2,1)} %param.4) | copy-start | bytes 1572868
  1.7 1.0 %copy-start.1 = (bf16[256,640]{1,0:T(8,128)(2,1)S(1)}, bf16[256,640]{1,0:T(8,128)(2,1)}, u32[]{:S(2)}) copy-start(bf16[256,640]{1,0:T(8,128)(2,1)} %teach_hbm.1) | copy-start | bytes 983044
  2.6 0.7 copy-start.2

commit v3 on v2

--- a/solution.py
+++ b/solution.py
@@ -248,13 +248,13 @@
         for b in range(2):
             rows = pl.ds(pl.multiple_of(row0 + b * 128, 128), 128)
             top = spread(t_fin[which, b : b + 1, :])
-            scale = KL_WEIGHT / spread(t_fin[which, 4 + b : 5 + b, :])
+            scale = GRAD_SCALE * KL_WEIGHT / spread(t_fin[which, 4 + b : 5 + b, :])
             label = spread(labels[b : b + 1, :])
             for n in range(COLS // 128):
                 at = slice(n * 128, (n + 1) * 128)
                 soft = jnp.exp(values[b * 128 : (b + 1) * 128, at].astype(F32) - top) * scale
                 ids = column_base + n * 128 + lax.broadcasted_iota(jnp.int32, (128, 128), 1)
-                base[c, rows, at] = soft + jnp.where(ids == label, 1.0 - KL_WEIGHT, 0.0)
+                base[c, rows, at] = soft + jnp.where(ids == label, GRAD_SCALE * (1.0 - KL_WEIGHT), 0.0)
         here = base.at[c, pl.ds(pl.multiple_of(row0, 256), 256), :]
         base_swaps.append(rdma(here, here, pr_s.at[2 + which], pr_r.at[2 + which], sib))
         base_swaps[-1].start()
@@ -276,13 +276,13 @@
     for which in range(2):
         tops = s_voc[0, 0:4, :] if which == 0 else s_voc[sib_slot, 0:4, :]
         core = c if which == 0 else 1 - c
-        factor = jnp.exp(tops - final[0:4, :]) / final[4:8, :]
+        factor = GRAD_SCALE * jnp.exp(tops - final[0:4, :]) / final[4:8, :]
         for b in range(4):
             rows = slice(b * 128, (b + 1) * 128)
             mat = spread(factor[b : b + 1, :])
             for n in range(COLS // 128):
                 at = slice(n * 128, (n + 1) * 128)
-                out = GRAD_SCALE * (prob[core, rows, at] * mat - base[core, rows, at])
+                out = prob[core, rows, at] * mat - base[core, rows, at]
                 grad[rows, which * COLS + n * 128 : which * COLS + (n + 1) * 128] = out.astype(BF16)
 
     def chunk_of(i):
@@ -387,8 +387,10 @@
             send_z(k, r).start()
         return carry
 
-    head_pieces(0, 4)
-    lax.fori_loop(0, 2, second, 0)
+    head_pieces(0, 3)
+    lax.fori_loop(0, 1, second, 0)
+    for copy in sends + base_swaps + [head_swap, lab_swap, teach_swap, fin_swap]:
+        copy.wait_send()
     for n in range(2):
         send_pair(n).wait_recv()
         total = own[6 + n] + pair_buf[n].astype(F32)
@@ -399,12 +401,35 @@
                 send_ya(2, r).start()
         else:
             send_xb(2).start()
-    head_pieces(4, 4)
-    lax.fori_loop(0, 2, third, 0)
-    head_pieces(8, 4)
+    lax.fori_loop(1, 2, second, 0)
+    head_pieces(3, 3)
+    lax.fori_loop(0, 1, third, 0)
+    head_pieces(6, 4)
+    lax.fori_loop(1, 2, third, 0)
     lax.fori_loop(2, 3, second, 0)
-    head_pieces(12, 4)
+    head_pieces(10, 4)
     lax.fori_loop(2, 3, third, 0)
+    head_pieces(14, 2)
+    prob_swap(0, xh).wait_send()
+    prob_swap(1, 1 - xh).wait_send()
+    for r in range(1, VOC):
+        stat_voc(t_voc, tv_s, tv_r, r).wait_send()
+        stat_voc(s_voc, sv_s, sv_r, r).wait_send()
+    for r in range(1, TOK):
+        stat_tok(t_tok, tt_s, tt_r, r).wait_send()
+        stat_tok(s_tok, st_s, st_r, r).wait_send()
+
+    def drain(k, carry):
+        for r in range(1, 4):
+            send_ya(k, r).wait_send()
+            send_yb(k, r).wait_send()
+        send_xa(k).wait_send()
+        send_xb(k).wait_send()
+        return carry
+
+    lax.fori_loop(0, 3, drain, 0)
+    for n in range(2):
+        send_pair(n).wait_send()
 
     z_rows = pl.ds(pl.multiple_of(z * 8, 8), 8)
     for k in range(3):
@@ -432,30 +457,14 @@
         hg_out[:, j * WIDE : (j + 1) * WIDE] = jnp.where(lower, mine, theirs).astype(BF16)
         hg_out[:, DHALF + j * WIDE : DHALF + (j + 1) * WIDE] = jnp.where(lower, theirs, mine).astype(BF16)
 
-    for copy in sends + base_swaps + [head_swap, lab_swap, teach_swap, fin_swap, fin_core]:
-        copy.wait_send()
-    prob_swap(0, xh).wait_send()
-    prob_swap(1, 1 - xh).wait_send()
-    for r in range(1, VOC):
-        stat_voc(t_voc, tv_s, tv_r, r).wait_send()
-        stat_voc(s_voc, sv_s, sv_r, r).wait_send()
-    for r in range(1, TOK):
-        stat_tok(t_tok, tt_s, tt_r, r).wait_send()
-        stat_tok(s_tok, st_s, st_r, r).wait_send()
-    for n in range(2):
-        send_pair(n).wait_send()
-
-    def drain(k, carry):
-        for r in range(1, 4):
-            send_ya(k, r).wait_send()
-            send_yb(k, r).wait_send()
-        send_xa(k).wait_send()
-        send_xb(k).wait_send()
+    fin_core.wait_send()
+
+    def drain_z(k, carry):
         for r in range(1, NZ):
             send_z(k, r).wait_send()
         return carry
 
-    lax.fori_loop(0, 3, drain, 0)
+    lax.fori_loop(0, 3, drain_z, 0)
 
     def drain_head(k, carry):
         ho_copy(k).wait()

time: 83.8 us -> 82.5 us (0.984)
  Pallas kernels: 77.3 us -> 76 us
    pallas_call x1, Pallas kernels: 77.3 us -> 76 us  [body(): pl.pallas_call(kernel, out_shape=(jax.ShapeDtypeStruct((4, 16 * WIDE), BF...]
where the time goes in v3:
time: 82.5 us; the launch traced here: 82.3 us
  Pallas kernels  76 us (92%)
  local copies, waits for them, and re-layouts  5.66 us (7%)
    pallas_call x1, Pallas kernels, body(): pl.pallas_call(kernel, out_shape=(jax.ShapeDtypeStruct((4, 16 * WIDE), BF...  76 us
    unnamed x8, local copies, waits for them, and re-layouts  5.66 us

profile of v3, /device:TPU:1, one launch (start us, length us, event | category | flops | bytes accessed | tf_op | source)
XLA Modules:
  0.0 82.3 jit_solution(5200066342333562322)
XLA Ops:
  0.6 0.0 copy-start
  0.6 1.0 %copy-done = bf16[1,64,4096]{2,1,0:T(8,128)(2,1)S(1)} copy-done((bf16[1,64,4096]{2,1,0:T(8,128)(2,1)S(1)}, bf16[1,64,4096]{2,1,0:T(8,128)(2,1)}, u32[]{:S(2)}) %copy-start) | copy-done | bytes 524312
  1.7 0.0 copy-start.1
  1.7 1.0 %copy-done.1 = bf16[256,640]{1,0:T(8,128)(2,1)S(1)} copy-done((bf16[256,640]{1,0:T(8,128)(2,1)S(1)}, bf16[256,640]{1,0:T(8,128)(2,1)}, u32[]{:S(2)}) %copy-start.1) | copy-done | bytes 327704
  2.6 0.0 copy-start.2
  2.6 0.7 copy-done.2
  3.3 76.0 %shard_map.59 = (bf16[4,4096]{1,0:T(4,128)(2,1)S(1)}, bf16[4096,640]{1,0:T(8,128)(2,1)S(1)}) custom-call(bf16[64,4096]{1,0:T(8,128)(2,1)S(1)} %bitcast.6, bf16[256,640]{1,0:T(8,128)(2,1)S(1)} %copy-done.1, s32[2,128]{1,0:T(2,128)S(1)} %bitcast.8, bf16[4096,640]{1,0:T(8,128)(2,1)} %bitcast.9), custom_call_target="tpu_custom_call" | custom-call | tf_op jit(solution)/shard_map/pallas_call | solution.py:507
  79.3 0.6 copy.8
  79.9 2.4 %copy.9 = bf16[1,4096,640]{2,1,0:T(8,128)(2,1)} copy(bf16[1,4096,640]{2,1,0:T(8,128)(2,1)S(1)} %bitcast.5) | data formatting | bytes 10485760
Async XLA Ops:
  0.6 1.0 %copy-start = (bf16[1,64,4096]{2,1,0:T(8,128)(2,1)S(1)}, bf16[1,64,4096]{2,1,0:T(8,128)(2,1)}, u32[]{:S(2)}) copy-start(bf16[1,64,4096]{2,1,0:T(8,128)(2,1)} %param.4) | copy-start | bytes 1572868
  1.7 1.0 %copy-start.1 = (bf16[256,640]{1,0:T(8,128)(2,1)S(1)}, bf16[256,640]{1,0:T(8,128)(2,1)}, u32[]{:S(2)}) copy-start(bf16[256,640]{1,0:T(8,128)(2,1)} %teach_hbm.1) | copy-start | bytes 983044
  2.6 0.7 copy-start.2

commit v4 on v3

--- a/solution.py
+++ b/solution.py
@@ -288,8 +288,13 @@
     def chunk_of(i):
         return jnp.where(i < 2, (1 - parity) * 2 + i, jnp.where(i < 6, i + 2, parity * 2 + i - 6))
 
-    def send_pair(i):
-        return rdma(part.at[i], pair_buf.at[i], pair_s.at[i], pair_r.at[i], zdev(1 if i == 0 else NZ - 1))
+    def send_pair_a(r):
+        yy = lax.rem(y + r, NY)
+        return rdma(part.at[0, :, yy], pair_buf.at[0, :, yy], pair_s.at[0, r], pair_r.at[0, r], zdev(1))
+
+    def send_pair_b(h):
+        col = 1 - xh if h == 0 else xh
+        return rdma(part.at[1, col], pair_buf.at[1, col], pair_s.at[1, h], pair_r.at[1, h], zdev(NZ - 1))
 
     def send_ya(k, r):
         return rdma(
@@ -339,7 +344,12 @@
 
             @pl.when(i == n)
             def _():
-                send_pair(n).start()
+                if n == 0:
+                    for r in (2, 1, 3, 0):
+                        send_pair_a(r).start()
+                else:
+                    for h in range(2):
+                        send_pair_b(h).start()
 
             @pl.when(i == 2 + 2 * n)
             def _():
@@ -387,20 +397,25 @@
             send_z(k, r).start()
         return carry
 
-    head_pieces(0, 3)
+    head_pieces(0, 2)
+    for r in (2, 1, 3):
+        send_pair_a(r).wait_recv()
+        yy = lax.rem(y + r, NY)
+        for col in range(2):
+            part[6, col, yy] = (own[6, col, yy] + pair_buf[0, col, yy].astype(F32)).astype(BF16)
+        send_ya(2, r).start()
+    send_pair_b(0).wait_recv()
+    part[7, 1 - xh] = (own[7, 1 - xh] + pair_buf[1, 1 - xh].astype(F32)).astype(BF16)
+    send_xb(2).start()
     lax.fori_loop(0, 1, second, 0)
+    send_pair_a(0).wait_recv()
+    for col in range(2):
+        own[6, col, y] = own[6, col, y] + pair_buf[0, col, y].astype(F32)
+    send_pair_b(1).wait_recv()
+    own[7, xh] = own[7, xh] + pair_buf[1, xh].astype(F32)
+    head_pieces(2, 1)
     for copy in sends + base_swaps + [head_swap, lab_swap, teach_swap, fin_swap]:
         copy.wait_send()
-    for n in range(2):
-        send_pair(n).wait_recv()
-        total = own[6 + n] + pair_buf[n].astype(F32)
-        own[6 + n] = total
-        part[6 + n] = total.astype(BF16)
-        if n == 0:
-            for r in (1, 3, 2):
-                send_ya(2, r).start()
-        else:
-            send_xb(2).start()
     lax.fori_loop(1, 2, second, 0)
     head_pieces(3, 3)
     lax.fori_loop(0, 1, third, 0)
@@ -428,8 +443,10 @@
         return carry
 
     lax.fori_loop(0, 3, drain, 0)
-    for n in range(2):
-        send_pair(n).wait_send()
+    for r in range(4):
+        send_pair_a(r).wait_send()
+    for h in range(2):
+        send_pair_b(h).wait_send()
 
     z_rows = pl.ds(pl.multiple_of(z * 8, 8), 8)
     for k in range(3):
@@ -498,7 +515,7 @@
         dma((7,)), dma((16,)), dma((48,)), dma((48,)), dma((5,)), dma((5,)),
         dma((VOC,)), dma((VOC,)), dma((TOK,)), dma((TOK,)),
         dma((VOC,)), dma((VOC,)), dma((TOK,)), dma((TOK,)),
-        dma((4,)), dma((4,)), dma((2,)), dma((2,)),
+        dma((4,)), dma((4,)), dma((2, 4)), dma((2, 4)),
         dma((3, 4)), dma((3, 4)), dma((3,)), dma((3,)),
         dma((3,)), dma((3,)), dma((3, 4)), dma((3, 4)),
         dma((3, NZ)), dma((3, NZ)),

time: 82.5 us -> 83.1 us (level)
  no operation moved by 1% of the time
where the time goes in v4:
time: 83.1 us; the launch traced here: 83 us
  Pallas kernels  76.6 us (92%)
  local copies, waits for them, and re-layouts  5.66 us (7%)
    pallas_call x1, Pallas kernels, body(): pl.pallas_call(kernel, out_shape=(jax.ShapeDtypeStruct((4, 16 * WIDE), BF...  76.6 us
    unnamed x8, local copies, waits for them, and re-layouts  5.66 us

profile of v4, /device:TPU:1, one launch (start us, length us, event | category | flops | bytes accessed | tf_op | source)
XLA Modules:
  0.0 83.0 jit_solution(1660859644160976175)
XLA Ops:
  0.6 0.0 copy-start
  0.6 1.0 %copy-done = bf16[1,64,4096]{2,1,0:T(8,128)(2,1)S(1)} copy-done((bf16[1,64,4096]{2,1,0:T(8,128)(2,1)S(1)}, bf16[1,64,4096]{2,1,0:T(8,128)(2,1)}, u32[]{:S(2)}) %copy-start) | copy-done | bytes 524312
  1.7 0.0 copy-start.1
  1.7 1.0 %copy-done.1 = bf16[256,640]{1,0:T(8,128)(2,1)S(1)} copy-done((bf16[256,640]{1,0:T(8,128)(2,1)S(1)}, bf16[256,640]{1,0:T(8,128)(2,1)}, u32[]{:S(2)}) %copy-start.1) | copy-done | bytes 327704
  2.6 0.0 copy-start.2
  2.6 0.7 copy-done.2
  3.3 76.6 %shard_map.59 = (bf16[4,4096]{1,0:T(4,128)(2,1)S(1)}, bf16[4096,640]{1,0:T(8,128)(2,1)S(1)}) custom-call(bf16[64,4096]{1,0:T(8,128)(2,1)S(1)} %bitcast.6, bf16[256,640]{1,0:T(8,128)(2,1)S(1)} %copy-done.1, s32[2,128]{1,0:T(2,128)S(1)} %bitcast.8, bf16[4096,640]{1,0:T(8,128)(2,1)} %bitcast.9), custom_call_target="tpu_custom_call" | custom-call | tf_op jit(solution)/shard_map/pallas_call | solution.py:524
  80.0 0.6 copy.8
  80.6 2.4 %copy.9 = bf16[1,4096,640]{2,1,0:T(8,128)(2,1)} copy(bf16[1,4096,640]{2,1,0:T(8,128)(2,1)S(1)} %bitcast.5) | data formatting | bytes 10485760
Async XLA Ops:
  0.6 1.0 %copy-start = (bf16[1,64,4096]{2,1,0:T(8,128)(2,1)S(1)}, bf16[1,64,4096]{2,1,0:T(8,128)(2,1)}, u32[]{:S(2)}) copy-start(bf16[1,64,4096]{2,1,0:T(8,128)(2,1)} %param.4) | copy-start | bytes 1572868
  1.7 1.0 %copy-start.1 = (bf16[256,640]{1,0:T(8,128)(2,1)S(1)}, bf16[256,640]{1,0:T(8,128)(2,1)}, u32[]{:S(2)}) copy-start(bf16[256,640]{1,0:T(8,128)(2,1)} %teach_hbm.1) | copy-start | bytes 983044
  2.6 0.7 copy-start.2
